TPU v7x, 32 devices: a whole 2x2x4 slice. The times are simulated.
32 devices in a mesh: groups: 2 (over x), tok: 16 (over z, y, core).
Axes of the slice: x: 2, y: 2, z: 4, core: 2. Of those that a mesh axis runs over, the one named last changes fastest.
Arguments:
- key_vectors: bfloat16 [4096, 4, 2048], P(('groups', 'tok')), parts along dimension 0, may hold values from -6 to 6
- beta_values: float32 [4096, 4, 16], P(('groups', 'tok')), parts along dimension 0, may hold values from 1 to 2
- gate_decay: float32 [4096, 16], P(('groups', 'tok')), parts along dimension 0, as said below
- input_rows: bfloat16 [4096, 2048], P(('groups', 'tok')), parts along dimension 0, may hold values from -0.3125 to 0.3125
- init_state: float32 [4096], P('groups'), parts along dimension 0, may hold values from -6 to 6
- w_out: bfloat16 [2048, 2048], P(None, 'tok'), may hold values from -0.125 to 0.125
Outputs:
- states: bfloat16 [4096, 2048], P(('groups', 'tok')), parts along dimension 0
- projected: bfloat16 [4096, 2048], P(('groups', 'tok')), parts along dimension 0
There are 2 independent parts, one for each index of `groups`. A program takes and returns all parts, laid end to end along the dimension named above; an argument that names none is the same for every part. Nothing has to cross between parts.
Inputs may be any that keep to these rules, and one draw needn't show every extreme that they name: `gate_decay`: decays are not negative.
All inputs are finite; a program needn't handle non-finite values.
Results may differ from a plain program's by a relative error of at most 0.0049.
Values may be sent and summed in bfloat16 or wider, within the bound.
A program may use at most 192 MiB of HBM per device.

v0:
```python
import jax
import jax.numpy as jnp
from jax import lax
from jax.sharding import PartitionSpec as P

BS = 128
REFL = 4


epsilon = 1e-06


def prefix(value, axis, join, neutral):
    count, mine = (lax.axis_size(axis), lax.axis_index(axis))
    pieces = jax.tree.map(lambda part: lax.all_gather(part, axis), value)
    total = jax.tree.map(
        lambda part, zero: jnp.full_like(part, 0) + jnp.asarray(zero, part.dtype), value, neutral
    )

    def turn(position, total):
        longer = join(total, jax.tree.map(lambda part: part[position], pieces))
        return jax.tree.map(lambda new, old: jnp.where(position < mine, new, old), longer, total)

    return lax.fori_loop(0, count - 1, turn, total)


def normalize(raw_keys):
    return raw_keys * lax.rsqrt(jnp.sum(raw_keys * raw_keys, axis=-1, keepdims=True) + epsilon)


def apply_maps(matrices, vectors):
    return jnp.einsum("bde,be->bd", matrices, vectors, precision=lax.Precision.HIGHEST)


def compose_maps(latter, earlier):
    return jnp.einsum("bde,bef->bdf", latter, earlier, precision=lax.Precision.HIGHEST)


def shards(key_vectors, beta_values, gate_decay, input_rows, init_state, w_out):
    highest = lax.Precision.HIGHEST
    tok_rows = key_vectors.shape[0]
    state_width = key_vectors.shape[2]
    blocks = state_width // BS
    window_len = 32
    windows = tok_rows // window_len
    refl_rows = REFL * window_len
    unit_keys = normalize(
        key_vectors.astype(jnp.float32).reshape(windows, window_len, REFL, blocks, BS)
    )
    reflect = unit_keys.transpose(3, 0, 1, 2, 4).reshape(blocks, windows, refl_rows, BS)
    strength = (
        beta_values.reshape(windows, window_len, REFL, blocks)
        .transpose(3, 0, 1, 2)
        .reshape(blocks, windows, refl_rows)
    )
    decay_rows = gate_decay.reshape(windows, window_len, blocks).transpose(2, 0, 1)
    token_pos = jnp.arange(window_len)
    up_to = (token_pos[None, :] <= token_pos[:, None]).astype(jnp.float32)
    refl_tok = jnp.arange(refl_rows) // REFL
    before_tok = (token_pos[None, :] < refl_tok[:, None]).astype(jnp.float32)
    through_tok = (refl_tok[None, :] <= token_pos[:, None]).astype(jnp.float32)
    cumulative = jnp.einsum("ts,bcs->bct", up_to, decay_rows, precision=highest)
    retain = jnp.exp(-cumulative)
    scaled_inputs = (
        input_rows.astype(jnp.float32)
        .reshape(windows, window_len, blocks, BS)
        .transpose(2, 0, 1, 3)
        / retain[..., None]
    )
    gram = jnp.einsum("bcrd,bcsd->bcrs", reflect, reflect, precision=highest)
    system = (
        jnp.tril(gram, -1) + jnp.eye(refl_rows, dtype=jnp.float32) * (1.0 / strength)[..., None]
    )
    solved = lax.linalg.triangular_solve(system, reflect, left_side=True, lower=True)
    pushed = jnp.sum(
        jnp.einsum("bcrd,bctd->bcrt", reflect, scaled_inputs, precision=highest) * before_tok,
        axis=-1,
    )
    weights_local = lax.linalg.triangular_solve(
        system, pushed[..., None], left_side=True, lower=True
    )[..., 0]
    removed = jnp.einsum(
        "tr,bcrd->bctd", through_tok, weights_local[..., None] * reflect, precision=highest
    )
    added = jnp.einsum("ts,bcsd->bctd", up_to, scaled_inputs, precision=highest)
    local_states = retain[..., None] * (added - removed)
    identity_block = jnp.eye(BS, dtype=jnp.float32)
    window_maps = retain[:, :, -1, None, None] * (
        identity_block - jnp.einsum("bcrd,bcre->bcde", reflect, solved, precision=highest)
    )
    per_window = window_maps.transpose(1, 0, 2, 3)
    window_ends = local_states[:, :, -1, :].transpose(1, 0, 2)

    def advance(running, pieces):
        return (apply_maps(pieces[0], running) + pieces[1], running)

    local_end, _ = lax.scan(
        advance, jnp.zeros((blocks, BS), jnp.float32), (per_window, window_ends)
    )

    def accumulate_maps(running, column_block):
        return (compose_maps(column_block, running), None)

    total_map, _ = lax.scan(
        accumulate_maps, jnp.broadcast_to(identity_block, (blocks, BS, BS)), per_window
    )
    start_state = init_state.reshape(blocks, BS)

    def combine(earlier, latter):
        return (compose_maps(latter[0], earlier[0]), apply_maps(latter[0], earlier[1]) + latter[1])

    neutral = (
        jnp.broadcast_to(identity_block, (blocks, BS, BS)),
        jnp.zeros((blocks, BS), jnp.float32),
    )
    prefix_map, prefix_vec = prefix((total_map, local_end), "tok", combine, neutral)
    entry_state = apply_maps(prefix_map, start_state) + prefix_vec
    _, starts = lax.scan(advance, entry_state, (per_window, window_ends))
    starts = starts.transpose(1, 0, 2)
    along_keys = jnp.einsum("bcre,bce->bcr", solved, starts, precision=highest)
    carried = starts[:, :, None, :] - jnp.einsum(
        "tr,bcrd->bctd", through_tok, along_keys[..., None] * reflect, precision=highest
    )
    full_states = local_states + retain[..., None] * carried
    states = full_states.transpose(1, 2, 0, 3).reshape(tok_rows, state_width).astype(jnp.bfloat16)
    projected = jnp.dot(
        states, lax.all_gather(w_out, "tok", axis=1, tiled=True), preferred_element_type=jnp.float32
    )
    return (states, projected.astype(jnp.bfloat16))


def solution(mesh):
    return jax.shard_map(
        shards,
        mesh=mesh,
        in_specs=(
            P(("groups", "tok"), None, None),
            P(("groups", "tok"), None, None),
            P(("groups", "tok"), None),
            P(("groups", "tok"), None),
            P("groups"),
            P(None, "tok"),
        ),
        out_specs=(P(("groups", "tok"), None), P(("groups", "tok"), None)),
        check_vma=False,
    )
```

profile of v0, /device:TPU:28, one launch (start us, length us, event | category | flops | bytes accessed | tf_op | source)
XLA Modules:
  0.0 959.0 jit_solution(16484867504410688511)
XLA Ops:
  7.3 4.7 reshape.120
  11.9 3.6 multiply_reduce_fusion
  16.9 3.6 copy.45
  21.1 14.3 %select_bitcast_fusion = f32[16,4,1,128,128]{4,3,2,1,0:T(8,128)} fusion(f32[16,4,128,128]{3,2,1,0:T(8,128)} %bitcast.185, f32[16,4,128]{2,1,0:T(4,128)S(1)} %copy.47, f32[128,128]{1,0:T(8,128)S(1)} %fusion.51, pred[128,128]{1,0:T(8,128)(4,1)S(1)} %get-tuple-element.291, pred[128,128]{1,0:T(8,128)(4,1)S(1)} %get-tuple-element.292), kind=kOutput, calls=%fused_computation.36 | convolution fusion | flops 1614807040 | bytes 8519680 | tf_op jit(solution)/shard_map/bcrd,bcsd->bcrs/dot_general | solution.py:70
  35.4 640.4 %custom-call.5 = f32[16,4,1,128,128]{3,4,2,1,0:T(8,128)} custom-call(f32[16,4,1,128,128]{4,3,2,1,0:T(8,128)} %select_bitcast_fusion), custom_call_target="InvertDiagBlocksLowerTriangular" | custom-call | tf_op jit(solution)/shard_map/triangular_solve | solution.py:79
  675.8 12.2 %fusion.20 = f32[16,4,128,128]{3,2,1,0:T(8,128)} fusion(f32[16,4,128,128]{3,2,1,0:T(8,128)} %bitcast.186, f32[16,4,1,128,128]{3,4,2,1,0:T(8,128)} %custom-call.5), kind=kOutput, calls=%fused_computation.28 | convolution fusion | flops 1610612736 | bytes 12582912 | tf_op jit(solution)/shard_map/triangular_solve | solution.py:74
  688.2 9.9 %bitcast_multiply_fusion = f32[4,16,128,128]{3,2,0,1:T(8,128)S(1)} fusion(f32[16,4,128,128]{3,2,1,0:T(8,128)} %bitcast.187, f32[16,4,128,128]{3,2,1,0:T(8,128)} %fusion.20, f32[4,16]{0,1:T(8,128)S(1)} %copy.48, f32[128,128]{1,0:T(8,128)S(1)} %fusion.51), kind=kOutput, calls=%fused_computation.27 | convolution fusion | flops 1612709888 | bytes 12648704 | tf_op jit(solution)/shard_map/bcrd,bcre->bcde/dot_general | solution.py:89
  700.8 10.2 %while.49 = (s32[]{:T(128)}, f32[16,128,128]{2,1,0:T(8,128)S(1)}, f32[4,16,128,128]{3,2,1,0:T(8,128)}, s32[]{:T(128)}) while((s32[]{:T(128)}, f32[16,128,128]{2,1,0:T(8,128)S(1)}, f32[4,16,128,128]{3,2,1,0:T(8,128)}, s32[]{:T(128)}) %tuple.89), condition=%wide.region_3.4_spmd, body=%wide.region_2.3_spmd.sunk | while | flops 402653184 | bytes 5243445 | solution.py:104
  715.1 6.9 fusion.48
  722.0 3.6 fusion.22
  728.2 12.0 %while.51 = (s32[]{:T(128)}, f32[16,128]{1,0:T(8,128)S(1)}, f32[4,16,128,128]{3,2,1,0:T(8,128)}, f32[4,16,128]{2,1,0:T(8,128)S(1)}, s32[]{:T(128)}, /*index=5*/s32[]{:T(128)}) while((s32[]{:T(128)}, f32[16,128]{1,0:T(8,128)S(1)}, f32[4,16,128,128]{3,2,1,0:T(8,128)}, f32[4,16,128]{2,1,0:T(8,128)S(1)}, s32[]{:T(128)}, ...), condition=%wide.region_5.6_spmd.clone, body=%wide.region_4.5_spmd.clone.sunk | while | flops 3149827 | bytes 1106515 | solution.py:97
  731.2 3.0 fusion.107
  734.2 3.0 fusion.107
  737.1 3.0 fusion.107
  740.1 17.4 %all-gather.1 = f32[256,128]{1,0:T(8,128)S(1)} all-gather(f32[16,128]{1,0:T(8,128)S(1)} %get-tuple-element.179), channel_id=3, replica_groups=mesh['groups'=2,'tok'=16] {'tok'}, dimensions={0}, use_global_device_ids=true | all-gather | bytes 139264 | tf_op jit(solution)/shard_map/all_gather | solution.py:15
  757.5 80.2 %all-gather.7.cloned.1.call-done = f32[256,128,128]{2,1,0:T(8,128)} async-done(((f32[16,128,128]{2,1,0:T(8,128)}), f32[256,128,128]{2,1,0:T(8,128)}) %all-gather.7.cloned.1.call-update) | async-done | bytes 16777232 | tf_op jit(solution)/shard_map/all_gather | solution.py:15
  837.9 83.2 %while.52 = (s32[]{:T(128)}, f32[16,128,128]{2,1,0:T(8,128)S(1)}, f32[16,128]{1,0:T(8,128)S(1)}, s32[]{:T(128)}, f32[16,16,128,128]{3,2,1,0:T(8,128)}, /*index=5*/f32[16,16,128]{2,1,0:T(8,128)S(1)}, s32[]{:T(128)}, s32[]{:T(128)}) while((s32[]{:T(128)}, f32[16,128,128]{2,1,0:T(8,128)S(1)}, f32[16,128]{1,0:T(8,128)S(1)}, s32[]{:T(128)}, ...), condition=%wide.region_7.8_spmd.clone, body=%wide.region_6.7_spmd.clone.sunk | while | flops 406069248 | bytes 7406703 | solution.py:24
  848.9 3.0 fusion.112
  865.6 3.0 fusion.112
  876.7 3.0 fusion.112
  922.8 11.9 %while.50 = (s32[]{:T(128)}, f32[16,128]{1,0:T(8,128)S(1)}, f32[4,16,128]{2,1,0:T(8,128)S(1)}, f32[4,16,128,128]{3,2,1,0:T(8,128)}, f32[4,16,128]{2,1,0:T(8,128)S(1)}, /*index=5*/s32[]{:T(128)}) while((s32[]{:T(128)}, f32[16,128]{1,0:T(8,128)S(1)}, f32[4,16,128]{2,1,0:T(8,128)S(1)}, f32[4,16,128,128]{3,2,1,0:T(8,128)}, ...), condition=%wide.region_9.10_spmd, body=%wide.region_8.9_spmd.sunk | while | flops 3147778 | bytes 1106509 | solution.py:118
  922.8 3.0 fusion.104
  934.7 8.5 fusion.53
  946.3 5.6 convolution_convert_fusion
  (160 shorter events, 111.8 us)
Async XLA Ops:
  7.2 913.9 %copy-start = (f32[2048]{0:T(1024)S(1)}, f32[2048]{0:T(1024)}, u32[]{:S(2)}) copy-start(f32[2048]{0:T(1024)} %param.18) | copy-start | bytes 24580
  7.2 830.6 %all-gather.7.cloned.1.call-start = ((), (), s32[]{:S(2)}) async-start(), calls=%async_computation.1 | async-start | bytes 17825792 | tf_op jit(solution)/shard_map/all_gather | solution.py:15
  11.9 3.7 copy-start.4
  16.8 3.6 copy-start.9
  16.8 3.9 copy-start.8
  700.8 12.1 %copy-start.7 = (bf16[128,2048]{1,0:T(8,128)(2,1)S(1)}, bf16[128,2048]{1,0:T(8,128)(2,1)}, u32[]{:S(2)}) copy-start(bf16[128,2048]{1,0:T(8,128)(2,1)} %param.17) | copy-start | bytes 1572868
  711.0 1.0 copy-start.3
  712.0 234.3 %all-gather.5.cloned.1.call-start = ((), (), s32[]{:S(2)}) async-start(), calls=%async_computation | async-start | bytes 8912896 | tf_op jit(solution)/shard_map/all_gather | solution.py:127
  712.9 2.2 copy-start.1
  713.2 8.8 copy-start.5
  934.6 8.5 copy-start.2
  946.3 5.7 copy-start.6
Sparse Core Ops, SparseCore 0:
  712.2 125.5 all-gather.6
  839.9 76.7 all-gather.4
where the time goes:
time: 968 us; the launch traced here: 959 us
  other arithmetic  646 us (67%)
  matrix products  183 us (19%)
  waiting for transfers between devices  80.6 us (8%)
  blocking collectives  17.4 us (2%)
  local copies, waits for them, and re-layouts  15.9 us (2%)
  between operations  14.6 us (2%)
    another operation x1, other arithmetic, shards(): lax.linalg.triangular_solve(system, pushed[..., None], left_side=True, lo...  640 us
    all_gather x1, waiting for transfers between devices, prefix(): pieces = jax.tree.map(lambda part: lax.all_gather(part, axis), value)  80.2 us
    dot_general x24, matrix products, apply_maps(): jnp.einsum('bde,be->bd', matrices, vectors, precision=lax.Precision.HIGHEST)  69.8 us
    dot_general x19, matrix products, compose_maps(): jnp.einsum('bde,bef->bdf', latter, earlier, precision=lax.Precision.HIGHEST)  46.4 us
  transfers between devices with their start and end apart: 2, of which 1 were waited for; matrix products, arithmetic and copies ran while one was open for 14% of the time, Pallas kernels for 0%

commit v1 on v0

v1 whole, which is shorter than its diff:
```python
import functools
import jax
import jax.numpy as jnp
from jax import lax
from jax.experimental import pallas as pl
from jax.experimental.pallas import tpu as pltpu
from jax.sharding import PartitionSpec as P

BS = 128
REFL = 4
WIN = BS // REFL
epsilon = 1e-06
F32 = jnp.float32
BF16 = jnp.bfloat16


def iota(shape, dim):
    return lax.broadcasted_iota(jnp.int32, shape, dim)


def split(a):
    high = a.astype(BF16)
    return high, (a - high.astype(F32)).astype(BF16)


def dot(a, b, dims=((1,), (0,))):
    return lax.dot_general(a, b, (dims, ((), ())), preferred_element_type=F32)


def dot3(a, b):
    (ah, al), (bh, bl) = a, b
    return dot(jnp.concatenate([ah, al, ah], 1), jnp.concatenate([bh, bh, bl], 0))


def to_col(row, eye):
    return jnp.sum(jnp.where(eye, row, 0.0), axis=1, keepdims=True)


def to_row(col, eye):
    return jnp.sum(jnp.where(eye, col, 0.0), axis=0, keepdims=True)


def local_kernel(per, windows, k_ref, vec_ref, v_ref, map_ref, end_ref, z_ref, z0_ref):
    i, j = iota((BS, BS), 0), iota((BS, BS), 1)
    eye = i == j
    eye_f = eye.astype(F32)
    tok, refl = iota((WIN, BS), 0), iota((WIN, BS), 1)
    systems = [(b, w) for b in range(per) for w in range(windows)]

    keys = {}
    a_mats, col_q, push, cums = {}, {}, {}, {}
    for b, w in systems:
        k = k_ref[w * BS : (w + 1) * BS, b * BS : (b + 1) * BS]
        v = v_ref[w * WIN : (w + 1) * WIN, b * BS : (b + 1) * BS]
        beta = vec_ref[b, w : w + 1, :]
        cum = vec_ref[b, windows + w : windows + w + 1, :]
        cum_col = to_col(cum, eye)
        tok_col = jnp.sum(jnp.where(refl == REFL * tok, cum, 0.0), axis=1, keepdims=True)
        gram = dot(k, k, ((1,), (1,)))
        q_row = beta / (to_row(gram, eye) + epsilon)
        q_col = to_col(q_row, eye)
        a_mats[b, w] = jnp.where(
            j < i, q_col * jnp.exp(jnp.minimum(cum - cum_col, 0.0)) * gram, 0.0
        )
        feed = dot(v, k, ((1,), (1,)))
        weigh = jnp.where(
            tok < refl // REFL, jnp.exp(jnp.minimum(tok_col - cum, 0.0)) * feed, 0.0
        )
        push[b, w] = q_row * jnp.sum(weigh, axis=0, keepdims=True)
        keys[b, w] = k
        col_q[b, w] = q_row * jnp.exp(-cum)
        cums[b, w] = (cum, cum_col, tok_col)

    inv = {s: jnp.where(eye, 1.0, jnp.where((i // 2 == j // 2), -a_mats[s], 0.0)) for s in systems}
    size = 2
    while size < BS:
        below = (i // (2 * size) == j // (2 * size)) & (i // size != j // size)
        for s in systems:
            t = split(inv[s])
            x = dot3(split(jnp.where(below, a_mats[s], 0.0)), t)
            inv[s] = inv[s] - dot3(t, split(x))
        size *= 2

    maps, ends = {}, {}
    for b, w in systems:
        s = (b, w)
        k = keys[s]
        cum, cum_col, tok_col = cums[s]
        cum_end = cum[:, BS - 1 : BS]
        th, tl = split(inv[s] * col_q[s])
        z = dot(jnp.concatenate([th, tl], 1), jnp.concatenate([k, k], 0))
        z0 = jnp.sum(inv[s] * push[s], axis=1, keepdims=True)
        z_ref[b, w] = z
        z0_ref[b, w : w + 1, :] = to_row(z0, eye)
        to_end = jnp.exp(cum_col - cum_end)
        eh, el = split(to_end * z)
        maps[s] = jnp.exp(-cum_end) * eye_f - dot(
            jnp.concatenate([eh, el], 0), jnp.concatenate([k, k], 0), ((0,), (0,))
        )
        v = v_ref[w * WIN : (w + 1) * WIN, b * BS : (b + 1) * BS].astype(F32)
        ends[s] = jnp.sum(jnp.exp(tok_col - cum_end) * v, axis=0, keepdims=True) - jnp.sum(
            (to_end * z0) * k.astype(F32), axis=0, keepdims=True
        )

    for b in range(per):
        end = ends[b, 0]
        total = maps[b, 0]
        for w in range(1, windows):
            end = jnp.sum(to_col(end, eye) * maps[b, w], axis=0, keepdims=True) + ends[b, w]
            total = dot3(split(total), split(maps[b, w]))
        map_ref[b] = total
        end_ref[b] = end


def chain_kernel(axis, map_ref, end_ref, init_ref, out_ref, held, going, send_sem, recv_sem):
    blocks = init_ref.shape[0]
    count, me = lax.axis_size(axis), lax.axis_index(axis)
    first, last = me == 0, me == count - 1
    barrier = pltpu.get_barrier_semaphore()

    @pl.when(jnp.logical_not(first))
    def _():
        pl.semaphore_signal(
            barrier, inc=1, device_id={axis: me - 1}, device_id_type=pl.DeviceIdType.MESH
        )

    @pl.when(jnp.logical_not(last))
    def _():
        pl.semaphore_signal(
            barrier, inc=1, device_id={axis: me + 1}, device_id_type=pl.DeviceIdType.MESH
        )

    pl.semaphore_wait(
        barrier, jnp.where(first, 0, 1).astype(jnp.int32) + jnp.where(last, 0, 1).astype(jnp.int32)
    )

    def copy(to):
        return pltpu.make_async_remote_copy(
            src_ref=going,
            dst_ref=held,
            send_sem=send_sem,
            recv_sem=recv_sem,
            device_id={axis: to},
            device_id_type=pl.DeviceIdType.MESH,
        )

    @pl.when(first)
    def _():
        out_ref[...] = init_ref[...]

    @pl.when(jnp.logical_not(first))
    def _():
        copy(lax.rem(me + 1, count)).wait_recv()
        out_ref[...] = held[...]

    @pl.when(jnp.logical_not(last))
    def _():
        columns = out_ref[...].T
        for b in range(blocks):
            going[b : b + 1, :] = (
                jnp.sum(columns[:, b : b + 1] * map_ref[b], axis=0, keepdims=True) + end_ref[b]
            )
        sending = copy(me + 1)
        sending.start()
        sending.wait_send()


def finish_kernel(per, windows, k_ref, vec_ref, v_ref, z_ref, z0_ref, x_ref, w_ref, s_ref, p_ref, acc):
    step = pl.program_id(0)
    eye = iota((BS, BS), 0) == iota((BS, BS), 1)
    tok, refl = iota((WIN, BS), 0), iota((WIN, BS), 1)
    ti, tj = iota((WIN, WIN), 0), iota((WIN, WIN), 1)
    now = [x_ref[b] for b in range(per)]
    for w in range(windows):
        for b in range(per):
            x = now[b]
            k = k_ref[w * BS : (w + 1) * BS, b * BS : (b + 1) * BS]
            v = v_ref[w * WIN : (w + 1) * WIN, b * BS : (b + 1) * BS]
            cum = vec_ref[b, windows + w : windows + w + 1, :]
            tok_col = jnp.sum(jnp.where(refl == REFL * tok, cum, 0.0), axis=1, keepdims=True)
            tok_row = to_row(tok_col, ti == tj)
            z = to_row(jnp.sum(z_ref[b, w] * x, axis=1, keepdims=True), eye) + z0_ref[b, w : w + 1, :]
            take = jnp.where(
                refl // REFL <= tok, jnp.exp(jnp.minimum(cum - tok_col, 0.0)) * z, 0.0
            )
            give = jnp.where(tj <= ti, jnp.exp(jnp.minimum(tok_row - tok_col, 0.0)), 0.0)
            th, tl = split(take)
            gh, gl = split(give)
            rows = (
                jnp.exp(-tok_col) * x
                + (dot(gh, v) + dot(gl, v))
                - dot(jnp.concatenate([th, tl], 1), jnp.concatenate([k, k], 0))
            )
            s_ref[w * WIN : (w + 1) * WIN, b * BS : (b + 1) * BS] = rows.astype(BF16)
            now[b] = rows[WIN - 1 : WIN, :]
    part = dot(s_ref[...], w_ref[...])

    @pl.when(step == 0)
    def _():
        acc[...] = part

    @pl.when(step > 0)
    def _():
        acc[...] += part

    @pl.when(step == pl.num_programs(0) - 1)
    def _():
        p_ref[...] = acc[...].astype(BF16)


def shards(key_vectors, beta_values, gate_decay, input_rows, init_state, w_out):
    tok_rows, _, width = key_vectors.shape
    blocks = width // BS
    windows = tok_rows // WIN
    refl_rows = REFL * tok_rows
    per = 2
    keys = key_vectors.reshape(refl_rows, width)
    pos = jnp.arange(WIN)
    up_to = (pos[None, :] <= pos[:, None]).astype(F32)
    cum = jnp.einsum(
        "ts,csb->bct", up_to, gate_decay.reshape(windows, WIN, blocks), precision=lax.Precision.HIGHEST
    )
    vec = jnp.concatenate(
        [
            beta_values.reshape(windows, BS, blocks).transpose(2, 0, 1),
            jnp.repeat(cum, REFL, axis=2),
        ],
        axis=1,
    )
    full_w = lax.all_gather(w_out, "tok", axis=1, tiled=True)
    vmem = 48 * 1024 * 1024
    key_spec = pl.BlockSpec((refl_rows, per * BS), lambda g: (0, g))
    vec_spec = pl.BlockSpec((per, 2 * windows, BS), lambda g: (g, 0, 0))
    row_spec = pl.BlockSpec((tok_rows, per * BS), lambda g: (0, g))
    z_spec = pl.BlockSpec((per, windows, BS, BS), lambda g: (g, 0, 0, 0))
    z0_spec = pl.BlockSpec((per, windows, BS), lambda g: (g, 0, 0))
    vector_spec = pl.BlockSpec((per, 1, BS), lambda g: (g, 0, 0))
    maps, ends, z, z0 = pl.pallas_call(
        functools.partial(local_kernel, per, windows),
        grid=(blocks // per,),
        in_specs=[key_spec, vec_spec, row_spec],
        out_specs=[pl.BlockSpec((per, BS, BS), lambda g: (g, 0, 0)), vector_spec, z_spec, z0_spec],
        out_shape=[
            jax.ShapeDtypeStruct((blocks, BS, BS), F32),
            jax.ShapeDtypeStruct((blocks, 1, BS), F32),
            jax.ShapeDtypeStruct((blocks, windows, BS, BS), F32),
            jax.ShapeDtypeStruct((blocks, windows, BS), F32),
        ],
        compiler_params=pltpu.CompilerParams(vmem_limit_bytes=vmem),
        cost_estimate=pl.CostEstimate(
            flops=blocks * windows * 45 * 2 * BS**3, bytes_accessed=10 << 20, transcendentals=0
        ),
        name="local",
    )(keys, vec, input_rows)
    whole = pl.BlockSpec(memory_space=pltpu.VMEM)
    entry = pl.pallas_call(
        functools.partial(chain_kernel, "tok"),
        in_specs=[whole] * 3,
        out_specs=whole,
        out_shape=jax.ShapeDtypeStruct((blocks, BS), F32),
        scratch_shapes=[
            pltpu.VMEM((blocks, BS), F32),
            pltpu.VMEM((blocks, BS), F32),
            pltpu.SemaphoreType.DMA,
            pltpu.SemaphoreType.DMA,
        ],
        compiler_params=pltpu.CompilerParams(
            collective_id=0, has_side_effects=True, vmem_limit_bytes=vmem
        ),
        cost_estimate=pl.CostEstimate(flops=60_000_000, bytes_accessed=60 << 20, transcendentals=0),
        name="chain",
    )(maps, ends, init_state.reshape(blocks, BS))
    out = w_out.shape[1] * lax.axis_size("tok")
    states, projected = pl.pallas_call(
        functools.partial(finish_kernel, per, windows),
        grid=(blocks // per,),
        in_specs=[
            key_spec,
            vec_spec,
            row_spec,
            z_spec,
            z0_spec,
            vector_spec,
            pl.BlockSpec((per * BS, out), lambda g: (g, 0)),
        ],
        out_specs=[row_spec, pl.BlockSpec((tok_rows, out), lambda g: (0, 0))],
        out_shape=[
            jax.ShapeDtypeStruct((tok_rows, width), BF16),
            jax.ShapeDtypeStruct((tok_rows, out), BF16),
        ],
        scratch_shapes=[pltpu.VMEM((tok_rows, out), F32)],
        compiler_params=pltpu.CompilerParams(vmem_limit_bytes=vmem),
        name="finish",
    )(keys, vec, input_rows, z, z0, entry.reshape(blocks, 1, BS), full_w)
    return (states, projected)


def solution(mesh):
    return jax.shard_map(
        shards,
        mesh=mesh,
        in_specs=(
            P(("groups", "tok"), None, None),
            P(("groups", "tok"), None, None),
            P(("groups", "tok"), None),
            P(("groups", "tok"), None),
            P("groups"),
            P(None, "tok"),
        ),
        out_specs=(P(("groups", "tok"), None), P(("groups", "tok"), None)),
        check_vma=False,
    )
```

time: 968 us -> 149 us (0.15)
  other arithmetic: 646 us -> 0.03 us
  matrix products: 183 us -> 0.14 us
  Pallas kernels: 0 us -> 130 us
  waiting for transfers between devices: 80.6 us -> 0.7 us
  blocking collectives: 17.4 us -> 0 us
  local copies, waits for them, and re-layouts: 15.9 us -> 3.13 us
    another operation x1 -> x0, other arithmetic: 640 us -> none  [shards(): lax.linalg.triangular_solve(system, pushed[..., None], left_side=True, lo...]
    dot_general x52 -> x0, matrix products: 167 us -> none  [the longest x24 69.8 us: apply_maps(): jnp.einsum('bde,be->bd', matrices, vectors, precision=lax.Precision.HIGHEST)]
    pallas_call x0 -> x3, Pallas kernels: none -> 130 us  [the longest x1 87.1 us: shards(): pl.pallas_call(functools.partial(local_kernel, per, windows), grid=(block...]
    all_gather x2 -> x1, waiting for transfers between devices: 80.3 us -> 0.02 us  [shards(): full_w = lax.all_gather(w_out, 'tok', axis=1, tiled=True)]
    all_gather x1 -> x0, blocking collectives: 17.4 us -> none  [prefix(): pieces = jax.tree.map(lambda part: lax.all_gather(part, axis), value)]
    another operation x2 -> x0, matrix products: 15.8 us -> none  [the longest x1 12.2 us: shards(): lax.linalg.triangular_solve(system, reflect, left_side=True, lower=True)]
  transfers between devices with their start and end apart: 2 -> 1, of which waited for: 1 -> 0; matrix products, arithmetic and copies ran while one was open for 14% -> 2% of each run, Pallas kernels for 0% -> 78%
where the time goes in v1:
time: 149 us; the launch traced here: 148 us
  Pallas kernels  130 us (87%)
  between operations  14.1 us (9%)
  local copies, waits for them, and re-layouts  3.13 us (2%)
    pallas_call x1, Pallas kernels, shards(): pl.pallas_call(functools.partial(local_kernel, per, windows), grid=(block...  87.1 us
    pallas_call x1, Pallas kernels, shards(): pl.pallas_call(functools.partial(chain_kernel, 'tok'), in_specs=[whole] *...  29.1 us
    pallas_call x1, Pallas kernels, shards(): pl.pallas_call(functools.partial(finish_kernel, per, windows), grid=(bloc...  13.9 us
  transfers between devices with their start and end apart: 1, of which 0 were waited for; matrix products, arithmetic and copies ran while one was open for 2% of the time, Pallas kernels for 78%

profile of v1, /device:TPU:28, one launch (start us, length us, event | category | flops | bytes accessed | tf_op | source)
XLA Modules:
  0.0 148.2 jit_solution(1478441379818388391)
XLA Ops:
  7.2 0.0 copy-start.3
  7.2 0.0 copy-start.2
  7.2 0.0 copy-start
  7.2 0.0 all-gather.2.cloned.1.call-start
  7.2 0.7 all-gather.2.cloned.1.call-update
  7.9 2.5 %reshape.22.k_ref = bf16[512,2048]{1,0:T(8,128)(2,1)S(1)} reshape(bf16[128,4,2048]{2,1,0:T(4,128)(2,1)} %param.6) | data formatting | bytes 4194304 | tf_op jit(solution)/shard_map/reshape | solution.py:217
  10.5 0.0 copy-done.3
  10.5 0.1 reshape.24
  10.6 0.1 fusion
  10.7 0.1 copy.14
  10.8 0.1 broadcast_in_dim.2
  10.9 0.1 copy.15
  11.0 0.0 copy-done.2
  11.0 0.2 copy.11
  11.1 0.1 copy.12
  11.3 0.0 copy-done
  11.3 0.0 copy-start.1
  11.3 87.1 %local.1 = (f32[16,128,128]{2,1,0:T(8,128)S(1)}, f32[16,1,128]{2,1,0:T(1,128)S(1)}, f32[16,4,128,128]{3,2,1,0:T(8,128)}, f32[16,4,128]{2,1,0:T(4,128)S(1)}) custom-call(bf16[512,2048]{1,0:T(8,128)(2,1)S(1)} %reshape.22.k_ref, f32[16,8,128]{2,1,0:T(8,128)S(1)} %pad_maximum_fusion.vec_ref, bf16[128,2048]{1,0:T(8,128)(2,1)S(1)} %copy-done), custom_call_target="tpu_custom_call" | custom-call | flops 12079595520 | bytes 10485760 | tf_op jit(solution)/shard_map/local/pallas_call | solution.py:238
  98.4 0.0 copy-done.1
  98.4 29.1 %chain.1 = f32[16,128]{1,0:T(8,128)S(1)} custom-call(f32[16,128,128]{2,1,0:T(8,128)S(1)} %get-tuple-element.8.map_ref, f32[16,1,128]{2,1,0:T(1,128)S(1)} %get-tuple-element.9.end_ref, f32[16,128]{1,0:T(8,128)S(1)} %bitcast.15), custom_call_target="tpu_custom_call" | custom-call | flops 60000000 | bytes 62914560 | tf_op jit(solution)/shard_map/chain/pallas_call | solution.py:256
  127.5 0.0 all-gather.2.cloned.1.call-done.w_ref
  127.5 13.9 %finish.1 = (bf16[128,2048]{1,0:T(8,128)(2,1)}, bf16[128,2048]{1,0:T(8,128)(2,1)}) custom-call(bf16[512,2048]{1,0:T(8,128)(2,1)S(1)} %reshape.22.k_ref, f32[16,8,128]{2,1,0:T(8,128)S(1)} %pad_maximum_fusion.vec_ref, bf16[128,2048]{1,0:T(8,128)(2,1)S(1)} %copy-done, f32[16,4,128,128]{3,2,1,0:T(8,128)} %get-tuple-element.6.z_ref, ...), custom_call_target="tpu_custom_call" | custom-call | tf_op jit(solution)/shard_map/finish/pallas_call | solution.py:274
  (2 shorter events, 0.0 us)
Async XLA Ops:
  7.2 3.3 %copy-start.3 = (f32[128,16]{0,1:T(8,128)S(1)}, f32[128,16]{0,1:T(8,128)}, u32[]{:S(2)}) copy-start(f32[128,16]{0,1:T(8,128)} %param.8) | copy-start | bytes 24580
  7.2 3.8 %copy-start.2 = (f32[128,4,16]{0,2,1:T(8,128)S(1)}, f32[128,4,16]{0,2,1:T(8,128)}, u32[]{:S(2)}) copy-start(f32[128,4,16]{0,2,1:T(8,128)} %param.7) | copy-start | bytes 98308
  7.2 4.1 %copy-start = (bf16[128,2048]{1,0:T(8,128)(2,1)S(1)}, bf16[128,2048]{1,0:T(8,128)(2,1)}, u32[]{:S(2)}) copy-start(bf16[128,2048]{1,0:T(8,128)(2,1)} %v_ref.3) | copy-start | bytes 1572868
  7.2 120.3 %all-gather.2.cloned.1.call-start = ((), (), s32[]{:S(2)}) async-start(), calls=%async_computation | async-start | bytes 8912896 | tf_op jit(solution)/shard_map/all_gather | solution.py:230
  11.3 87.2 %copy-start.1 = (f32[2048]{0:T(1024)S(1)}, f32[2048]{0:T(1024)}, u32[]{:S(2)}) copy-start(f32[2048]{0:T(1024)} %param.10) | copy-start | bytes 24580
Sparse Core Ops, SparseCore 0:
  10.2 76.6 all-gather.1

commit v2 on v1

--- a/solution.py
+++ b/solution.py
@@ -29,7 +29,7 @@
 
 def dot3(a, b):
     (ah, al), (bh, bl) = a, b
-    return dot(jnp.concatenate([ah, al, ah], 1), jnp.concatenate([bh, bh, bl], 0))
+    return dot(ah, bh) + (dot(al, bh) + dot(ah, bl))
 
 
 def to_col(row, eye):
@@ -88,14 +88,14 @@
         cum, cum_col, tok_col = cums[s]
         cum_end = cum[:, BS - 1 : BS]
         th, tl = split(inv[s] * col_q[s])
-        z = dot(jnp.concatenate([th, tl], 1), jnp.concatenate([k, k], 0))
+        z = (dot(th, k) + dot(tl, k))
         z0 = jnp.sum(inv[s] * push[s], axis=1, keepdims=True)
         z_ref[b, w] = z
         z0_ref[b, w : w + 1, :] = to_row(z0, eye)
         to_end = jnp.exp(cum_col - cum_end)
         eh, el = split(to_end * z)
-        maps[s] = jnp.exp(-cum_end) * eye_f - dot(
-            jnp.concatenate([eh, el], 0), jnp.concatenate([k, k], 0), ((0,), (0,))
+        maps[s] = jnp.exp(-cum_end) * eye_f - (
+            dot(eh, k, ((0,), (0,))) + dot(el, k, ((0,), (0,)))
         )
         v = v_ref[w * WIN : (w + 1) * WIN, b * BS : (b + 1) * BS].astype(F32)
         ends[s] = jnp.sum(jnp.exp(tok_col - cum_end) * v, axis=0, keepdims=True) - jnp.sum(
@@ -189,7 +189,7 @@
             rows = (
                 jnp.exp(-tok_col) * x
                 + (dot(gh, v) + dot(gl, v))
-                - dot(jnp.concatenate([th, tl], 1), jnp.concatenate([k, k], 0))
+                - (dot(th, k) + dot(tl, k))
             )
             s_ref[w * WIN : (w + 1) * WIN, b * BS : (b + 1) * BS] = rows.astype(BF16)
             now[b] = rows[WIN - 1 : WIN, :]

time: 149 us -> 112 us (0.75)
  the two profiles are of different devices: /device:TPU:28 before, /device:TPU:0 now
where the time goes in v2:
time: 112 us
  Pallas kernels  51.6 us (46%)
  waiting for transfers between devices  43.1 us (38%)
  between operations  14.1 us (13%)
  local copies, waits for them, and re-layouts  3.14 us (3%)
    all_gather x1, waiting for transfers between devices, shards(): full_w = lax.all_gather(w_out, 'tok', axis=1, tiled=True)  42.4 us
    pallas_call x1, Pallas kernels, shards(): pl.pallas_call(functools.partial(local_kernel, per, windows), grid=(block...  35.7 us
    pallas_call x1, Pallas kernels, shards(): pl.pallas_call(functools.partial(finish_kernel, per, windows), grid=(bloc...  14.2 us
    reshape x1, local copies, waits for them, and re-layouts, shards(): keys = key_vectors.reshape(refl_rows, width)  2.54 us
  transfers between devices with their start and end apart: 1, of which 1 were waited for; matrix products, arithmetic and copies ran while one was open for 3% of the time, Pallas kernels for 33%

profile of v2, /device:TPU:0, one launch (start us, length us, event | category | flops | bytes accessed | tf_op | source)
XLA Modules:
  0.0 112.2 jit_solution(6254597245242027034)
XLA Ops:
  7.2 0.0 copy-start.3
  7.2 0.0 copy-start.2
  7.2 0.0 copy-start
  7.2 0.0 all-gather.2.cloned.1.call-start
  7.2 0.7 all-gather.2.cloned.1.call-update
  7.9 2.5 %reshape.22.k_ref = bf16[512,2048]{1,0:T(8,128)(2,1)S(1)} reshape(bf16[128,4,2048]{2,1,0:T(4,128)(2,1)} %param.6) | data formatting | bytes 4194304 | tf_op jit(solution)/shard_map/reshape | solution.py:217
  10.5 0.0 copy-done.3
  10.5 0.1 reshape.24
  10.6 0.1 fusion
  10.7 0.1 copy.14
  10.8 0.1 broadcast_in_dim.2
  10.9 0.1 copy.15
  11.0 0.0 copy-done.2
  11.0 0.2 copy.11
  11.1 0.1 copy.12
  11.3 0.0 copy-done
  11.3 0.0 copy-start.1
  11.3 35.7 %local.1 = (f32[16,128,128]{2,1,0:T(8,128)S(1)}, f32[16,1,128]{2,1,0:T(1,128)S(1)}, f32[16,4,128,128]{3,2,1,0:T(8,128)}, f32[16,4,128]{2,1,0:T(4,128)S(1)}) custom-call(bf16[512,2048]{1,0:T(8,128)(2,1)S(1)} %reshape.22.k_ref, f32[16,8,128]{2,1,0:T(8,128)S(1)} %pad_maximum_fusion.vec_ref, bf16[128,2048]{1,0:T(8,128)(2,1)S(1)} %copy-done), custom_call_target="tpu_custom_call" | custom-call | flops 12079595520 | bytes 10485760 | tf_op jit(solution)/shard_map/local/pallas_call | solution.py:238
  47.0 0.0 copy-done.1
  47.0 1.8 %chain.1 = f32[16,128]{1,0:T(8,128)S(1)} custom-call(f32[16,128,128]{2,1,0:T(8,128)S(1)} %get-tuple-element.8.map_ref, f32[16,1,128]{2,1,0:T(1,128)S(1)} %get-tuple-element.9.end_ref, f32[16,128]{1,0:T(8,128)S(1)} %bitcast.15), custom_call_target="tpu_custom_call" | custom-call | flops 60000000 | bytes 62914560 | tf_op jit(solution)/shard_map/chain/pallas_call | solution.py:256
  48.8 42.4 %all-gather.2.cloned.1.call-done.w_ref = bf16[2048,2048]{1,0:T(8,128)(2,1)} async-done(((bf16[2048,128]{1,0:T(8,128)(2,1)}), bf16[2048,2048]{1,0:T(8,128)(2,1)}) %all-gather.2.cloned.1.call-update) | async-done | bytes 8388624 | tf_op jit(solution)/shard_map/all_gather | solution.py:230
  91.2 14.2 %finish.1 = (bf16[128,2048]{1,0:T(8,128)(2,1)}, bf16[128,2048]{1,0:T(8,128)(2,1)}) custom-call(bf16[512,2048]{1,0:T(8,128)(2,1)S(1)} %reshape.22.k_ref, f32[16,8,128]{2,1,0:T(8,128)S(1)} %pad_maximum_fusion.vec_ref, bf16[128,2048]{1,0:T(8,128)(2,1)S(1)} %copy-done, f32[16,4,128,128]{3,2,1,0:T(8,128)} %get-tuple-element.6.z_ref, ...), custom_call_target="tpu_custom_call" | custom-call | tf_op jit(solution)/shard_map/finish/pallas_call | solution.py:274
  (2 shorter events, 0.0 us)
Async XLA Ops:
  7.2 3.3 %copy-start.3 = (f32[128,16]{0,1:T(8,128)S(1)}, f32[128,16]{0,1:T(8,128)}, u32[]{:S(2)}) copy-start(f32[128,16]{0,1:T(8,128)} %param.8) | copy-start | bytes 24580
  7.2 3.8 %copy-start.2 = (f32[128,4,16]{0,2,1:T(8,128)S(1)}, f32[128,4,16]{0,2,1:T(8,128)}, u32[]{:S(2)}) copy-start(f32[128,4,16]{0,2,1:T(8,128)} %param.7) | copy-start | bytes 98308
  7.2 4.1 %copy-start = (bf16[128,2048]{1,0:T(8,128)(2,1)S(1)}, bf16[128,2048]{1,0:T(8,128)(2,1)}, u32[]{:S(2)}) copy-start(bf16[128,2048]{1,0:T(8,128)(2,1)} %v_ref.3) | copy-start | bytes 1572868
  7.2 84.0 %all-gather.2.cloned.1.call-start = ((), (), s32[]{:S(2)}) async-start(), calls=%async_computation | async-start | bytes 8912896 | tf_op jit(solution)/shard_map/all_gather | solution.py:230
  11.3 35.7 %copy-start.1 = (f32[2048]{0:T(1024)S(1)}, f32[2048]{0:T(1024)}, u32[]{:S(2)}) copy-start(f32[2048]{0:T(1024)} %param.10) | copy-start | bytes 24580
Sparse Core Ops, SparseCore 0:
  10.2 80.9 all-gather.1

commit v3 on v2

--- a/solution.py
+++ b/solution.py
@@ -165,7 +165,7 @@
         sending.wait_send()
 
 
-def finish_kernel(per, windows, k_ref, vec_ref, v_ref, z_ref, z0_ref, x_ref, w_ref, s_ref, p_ref, acc):
+def finish_kernel(per, windows, strip, k_ref, vec_ref, v_ref, z_ref, z0_ref, x_ref, w_ref, s_ref, p_ref, acc):
     step = pl.program_id(0)
     eye = iota((BS, BS), 0) == iota((BS, BS), 1)
     tok, refl = iota((WIN, BS), 0), iota((WIN, BS), 1)
@@ -193,19 +193,26 @@
             )
             s_ref[w * WIN : (w + 1) * WIN, b * BS : (b + 1) * BS] = rows.astype(BF16)
             now[b] = rows[WIN - 1 : WIN, :]
-    part = dot(s_ref[...], w_ref[...])
-
-    @pl.when(step == 0)
-    def _():
-        acc[...] = part
-
-    @pl.when(step > 0)
-    def _():
-        acc[...] += part
+    half = w_ref.shape[2]
+    rows = s_ref[...]
+    for side in range(2):
+        part = dot(rows, w_ref[side])
+
+        @pl.when(step == 0)
+        def _():
+            acc[side] = part
+
+        @pl.when(step > 0)
+        def _():
+            acc[side] += part
 
     @pl.when(step == pl.num_programs(0) - 1)
     def _():
-        p_ref[...] = acc[...].astype(BF16)
+        for at in range(half // strip):
+            for side in range(2):
+                p_ref[:, (2 * at + side) * strip : (2 * at + side + 1) * strip] = acc[
+                    side, :, at * strip : (at + 1) * strip
+                ].astype(BF16)
 
 
 def shards(key_vectors, beta_values, gate_decay, input_rows, init_state, w_out):
@@ -227,7 +234,11 @@
         ],
         axis=1,
     )
-    full_w = lax.all_gather(w_out, "tok", axis=1, tiled=True)
+    count = lax.axis_size("tok")
+    same_core = [list(range(core, count, 2)) for core in range(2)]
+    same_chip = [[2 * chip, 2 * chip + 1] for chip in range(count // 2)]
+    half_w = lax.all_gather(w_out, "tok", axis=1, tiled=True, axis_index_groups=same_core)
+    full_w = lax.all_gather(half_w, "tok", axis=0, axis_index_groups=same_chip)
     vmem = 48 * 1024 * 1024
     key_spec = pl.BlockSpec((refl_rows, per * BS), lambda g: (0, g))
     vec_spec = pl.BlockSpec((per, 2 * windows, BS), lambda g: (g, 0, 0))
@@ -271,8 +282,9 @@
         name="chain",
     )(maps, ends, init_state.reshape(blocks, BS))
     out = w_out.shape[1] * lax.axis_size("tok")
+    strip = w_out.shape[1] if w_out.shape[1] % BS == 0 else out // 2
     states, projected = pl.pallas_call(
-        functools.partial(finish_kernel, per, windows),
+        functools.partial(finish_kernel, per, windows, strip),
         grid=(blocks // per,),
         in_specs=[
             key_spec,
@@ -281,17 +293,23 @@
             z_spec,
             z0_spec,
             vector_spec,
-            pl.BlockSpec((per * BS, out), lambda g: (g, 0)),
+            pl.BlockSpec((2, per * BS, out // 2), lambda g: (0, g, 0)),
         ],
         out_specs=[row_spec, pl.BlockSpec((tok_rows, out), lambda g: (0, 0))],
         out_shape=[
             jax.ShapeDtypeStruct((tok_rows, width), BF16),
             jax.ShapeDtypeStruct((tok_rows, out), BF16),
         ],
-        scratch_shapes=[pltpu.VMEM((tok_rows, out), F32)],
+        scratch_shapes=[pltpu.VMEM((2, tok_rows, out // 2), F32)],
         compiler_params=pltpu.CompilerParams(vmem_limit_bytes=vmem),
         name="finish",
     )(keys, vec, input_rows, z, z0, entry.reshape(blocks, 1, BS), full_w)
+    if strip != w_out.shape[1]:
+        projected = (
+            projected.reshape(tok_rows, 2, count // 2, w_out.shape[1])
+            .transpose(0, 2, 1, 3)
+            .reshape(tok_rows, out)
+        )
     return (states, projected)
 
 

time: 112 us -> 177 us (1.58)
  the two profiles are of different devices: /device:TPU:0 before, /device:TPU:28 now
where the time goes in v3:
time: 177 us
  Pallas kernels  83.3 us (47%)
  waiting for transfers between devices  76 us (43%)
  between operations  14.1 us (8%)
  local copies, waits for them, and re-layouts  3.14 us (2%)
    all_gather x1, waiting for transfers between devices, shards(): lax.all_gather(w_out, 'tok', axis=1, tiled=True, axis_index_groups=same_c...  75.3 us
    pallas_call x1, Pallas kernels, shards(): pl.pallas_call(functools.partial(local_kernel, per, windows), grid=(block...  35.7 us
    pallas_call x1, Pallas kernels, shards(): pl.pallas_call(functools.partial(chain_kernel, 'tok'), in_specs=[whole] *...  32.2 us
    pallas_call x1, Pallas kernels, shards(): pl.pallas_call(functools.partial(finish_kernel, per, windows, strip), gri...  15.4 us
  transfers between devices with their start and end apart: 2, of which 1 were waited for; matrix products, arithmetic and copies ran while one was open for 2% of the time, Pallas kernels for 38%

profile of v3, /device:TPU:28, one launch (start us, length us, event | category | flops | bytes accessed | tf_op | source)
XLA Modules:
  0.0 176.8 jit_solution(6341043737243840651)
XLA Ops:
  7.2 0.0 copy-start.3
  7.2 0.0 copy-start.2
  7.2 0.0 all-gather.4.cloned.1.call-start
  7.2 0.7 all-gather.4.cloned.1.call-update
  7.9 0.0 all-gather.6.cloned.1.call-start
  8.0 75.3 %all-gather.4.cloned.1.call-done = bf16[2048,1024]{1,0:T(8,128)(2,1)} async-done(((bf16[2048,128]{1,0:T(8,128)(2,1)}), bf16[2048,1024]{1,0:T(8,128)(2,1)}) %all-gather.4.cloned.1.call-update) | async-done | bytes 4194320 | tf_op jit(solution)/shard_map/all_gather | solution.py:240
  83.2 0.0 all-gather.6.cloned.1.call-update
  83.2 0.0 copy-done.3
  83.3 0.1 reshape.24
  83.4 0.1 fusion
  83.5 0.1 copy.14
  83.6 0.1 broadcast_in_dim.2
  83.6 0.1 copy.15
  83.7 0.0 copy-done.2
  83.7 0.2 copy.11
  83.9 0.1 copy.12
  84.0 2.5 %reshape.22.k_ref = bf16[512,2048]{1,0:T(8,128)(2,1)S(1)} reshape(bf16[128,4,2048]{2,1,0:T(4,128)(2,1)} %param.6) | data formatting | bytes 4194304 | tf_op jit(solution)/shard_map/reshape | solution.py:224
  86.6 0.0 copy-done
  86.6 0.0 copy-start.1
  86.6 35.7 %local.1 = (f32[16,128,128]{2,1,0:T(8,128)S(1)}, f32[16,1,128]{2,1,0:T(1,128)S(1)}, f32[16,4,128,128]{3,2,1,0:T(8,128)}, f32[16,4,128]{2,1,0:T(4,128)S(1)}) custom-call(bf16[512,2048]{1,0:T(8,128)(2,1)S(1)} %reshape.22.k_ref, f32[16,8,128]{2,1,0:T(8,128)S(1)} %pad_maximum_fusion.vec_ref, bf16[128,2048]{1,0:T(8,128)(2,1)S(1)} %copy-done), custom_call_target="tpu_custom_call" | custom-call | flops 12079595520 | bytes 10485760 | tf_op jit(solution)/shard_map/local/pallas_call | solution.py:249
  122.3 0.0 copy-done.1
  122.3 32.2 %chain.1 = f32[16,128]{1,0:T(8,128)S(1)} custom-call(f32[16,128,128]{2,1,0:T(8,128)S(1)} %get-tuple-element.8.map_ref, f32[16,1,128]{2,1,0:T(1,128)S(1)} %get-tuple-element.9.end_ref, f32[16,128]{1,0:T(8,128)S(1)} %bitcast.16), custom_call_target="tpu_custom_call" | custom-call | flops 60000000 | bytes 62914560 | tf_op jit(solution)/shard_map/chain/pallas_call | solution.py:267
  154.5 0.0 all-gather.6.cloned.1.call-done
  154.5 15.4 %finish.1 = (bf16[128,2048]{1,0:T(8,128)(2,1)}, bf16[128,2048]{1,0:T(8,128)(2,1)}) custom-call(bf16[512,2048]{1,0:T(8,128)(2,1)S(1)} %reshape.22.k_ref, f32[16,8,128]{2,1,0:T(8,128)S(1)} %pad_maximum_fusion.vec_ref, bf16[128,2048]{1,0:T(8,128)(2,1)S(1)} %copy-done, f32[16,4,128,128]{3,2,1,0:T(8,128)} %get-tuple-element.6.z_ref, ...), custom_call_target="tpu_custom_call" | custom-call | tf_op jit(solution)/shard_map/finish/pallas_call | solution.py:286
  (3 shorter events, 0.0 us)
Async XLA Ops:
  7.2 76.1 %copy-start.3 = (f32[128,16]{0,1:T(8,128)S(1)}, f32[128,16]{0,1:T(8,128)}, u32[]{:S(2)}) copy-start(f32[128,16]{0,1:T(8,128)} %param.8) | copy-start | bytes 24580
  7.2 76.6 %copy-start.2 = (f32[128,4,16]{0,2,1:T(8,128)S(1)}, f32[128,4,16]{0,2,1:T(8,128)}, u32[]{:S(2)}) copy-start(f32[128,4,16]{0,2,1:T(8,128)} %param.7) | copy-start | bytes 98308
  7.2 76.0 %all-gather.4.cloned.1.call-start = ((), (), s32[]{:S(2)}) async-start(), calls=%async_computation | async-start | bytes 4718592 | tf_op jit(solution)/shard_map/all_gather | solution.py:240
  7.9 146.6 %all-gather.6.cloned.1.call-start = ((), (), s32[]{:S(2)}) async-start(), calls=%async_computation.1 | async-start | bytes 12582912 | tf_op jit(solution)/shard_map/all_gather | solution.py:241
  83.2 3.4 %copy-start = (bf16[128,2048]{1,0:T(8,128)(2,1)S(1)}, bf16[128,2048]{1,0:T(8,128)(2,1)}, u32[]{:S(2)}) copy-start(bf16[128,2048]{1,0:T(8,128)(2,1)} %v_ref.3) | copy-start | bytes 1572868
  86.6 35.7 %copy-start.1 = (f32[2048]{0:T(1024)S(1)}, f32[2048]{0:T(1024)}, u32[]{:S(2)}) copy-start(f32[2048]{0:T(1024)} %param.10) | copy-start | bytes 24580
Sparse Core Ops, SparseCore 0:
  10.1 73.1 all-gather.3
  84.8 21.1 all-gather.5

commit v4 on v2

--- a/solution.py
+++ b/solution.py
@@ -165,8 +165,7 @@
         sending.wait_send()
 
 
-def finish_kernel(per, windows, k_ref, vec_ref, v_ref, z_ref, z0_ref, x_ref, w_ref, s_ref, p_ref, acc):
-    step = pl.program_id(0)
+def states_kernel(per, windows, k_ref, vec_ref, v_ref, z_ref, z0_ref, x_ref, s_ref):
     eye = iota((BS, BS), 0) == iota((BS, BS), 1)
     tok, refl = iota((WIN, BS), 0), iota((WIN, BS), 1)
     ti, tj = iota((WIN, WIN), 0), iota((WIN, WIN), 1)
@@ -193,19 +192,6 @@
             )
             s_ref[w * WIN : (w + 1) * WIN, b * BS : (b + 1) * BS] = rows.astype(BF16)
             now[b] = rows[WIN - 1 : WIN, :]
-    part = dot(s_ref[...], w_ref[...])
-
-    @pl.when(step == 0)
-    def _():
-        acc[...] = part
-
-    @pl.when(step > 0)
-    def _():
-        acc[...] += part
-
-    @pl.when(step == pl.num_programs(0) - 1)
-    def _():
-        p_ref[...] = acc[...].astype(BF16)
 
 
 def shards(key_vectors, beta_values, gate_decay, input_rows, init_state, w_out):
@@ -270,28 +256,27 @@
         cost_estimate=pl.CostEstimate(flops=60_000_000, bytes_accessed=60 << 20, transcendentals=0),
         name="chain",
     )(maps, ends, init_state.reshape(blocks, BS))
-    out = w_out.shape[1] * lax.axis_size("tok")
-    states, projected = pl.pallas_call(
-        functools.partial(finish_kernel, per, windows),
-        grid=(blocks // per,),
+    more = 4
+    states = pl.pallas_call(
+        functools.partial(states_kernel, more, windows),
+        grid=(blocks // more,),
         in_specs=[
-            key_spec,
-            vec_spec,
-            row_spec,
-            z_spec,
-            z0_spec,
-            vector_spec,
-            pl.BlockSpec((per * BS, out), lambda g: (g, 0)),
-        ],
-        out_specs=[row_spec, pl.BlockSpec((tok_rows, out), lambda g: (0, 0))],
-        out_shape=[
-            jax.ShapeDtypeStruct((tok_rows, width), BF16),
-            jax.ShapeDtypeStruct((tok_rows, out), BF16),
-        ],
-        scratch_shapes=[pltpu.VMEM((tok_rows, out), F32)],
+            pl.BlockSpec((refl_rows, more * BS), lambda g: (0, g)),
+            pl.BlockSpec((more, 2 * windows, BS), lambda g: (g, 0, 0)),
+            pl.BlockSpec((tok_rows, more * BS), lambda g: (0, g)),
+            pl.BlockSpec((more, windows, BS, BS), lambda g: (g, 0, 0, 0)),
+            pl.BlockSpec((more, windows, BS), lambda g: (g, 0, 0)),
+            pl.BlockSpec((more, 1, BS), lambda g: (g, 0, 0)),
+        ],
+        out_specs=pl.BlockSpec((tok_rows, more * BS), lambda g: (0, g)),
+        out_shape=jax.ShapeDtypeStruct((tok_rows, width), BF16),
         compiler_params=pltpu.CompilerParams(vmem_limit_bytes=vmem),
-        name="finish",
-    )(keys, vec, input_rows, z, z0, entry.reshape(blocks, 1, BS), full_w)
+        cost_estimate=pl.CostEstimate(
+            flops=blocks * windows * 8 * BS**3, bytes_accessed=10 << 20, transcendentals=0
+        ),
+        name="states",
+    )(keys, vec, input_rows, z, z0, entry.reshape(blocks, 1, BS))
+    projected = jnp.dot(states, full_w, preferred_element_type=F32).astype(BF16)
     return (states, projected)
 
 

time: 112 us -> 104 us (0.929)
  waiting for transfers between devices: 43.1 us -> 33.8 us
  Pallas kernels: 51.6 us -> 44.2 us
  matrix products: 0.15 us -> 5.77 us
  local copies, waits for them, and re-layouts: 3.14 us -> 5.62 us
    all_gather x1, waiting for transfers between devices: 42.4 us -> 33.2 us  [shards(): full_w = lax.all_gather(w_out, 'tok', axis=1, tiled=True)]
    pallas_call x1, Pallas kernels: 14.2 us -> 6.72 us  [shards(): pl.pallas_call(functools.partial(states_kernel, more, windows), grid=(blo...]
    dot_general x0 -> x1, matrix products: none -> 5.62 us  [shards(): projected = jnp.dot(states, full_w, preferred_element_type=F32).astype(BF16)]
    unnamed x9 -> x7, local copies, waits for them, and re-layouts: 0.18 us -> 1.96 us
  transfers between devices with their start and end apart: 1 -> 1, of which waited for: 1 -> 1; matrix products, arithmetic and copies ran while one was open for 3% -> 5% of each run, Pallas kernels for 33% -> 43%
where the time goes in v4:
time: 104 us
  Pallas kernels  44.2 us (42%)
  waiting for transfers between devices  33.8 us (32%)
  between operations  14.1 us (14%)
  matrix products  5.77 us (6%)
  local copies, waits for them, and re-layouts  5.62 us (5%)
    pallas_call x1, Pallas kernels, shards(): pl.pallas_call(functools.partial(local_kernel, per, windows), grid=(block...  35.7 us
    all_gather x1, waiting for transfers between devices, shards(): full_w = lax.all_gather(w_out, 'tok', axis=1, tiled=True)  33.2 us
    pallas_call x1, Pallas kernels, shards(): pl.pallas_call(functools.partial(states_kernel, more, windows), grid=(blo...  6.72 us
    dot_general x1, matrix products, shards(): projected = jnp.dot(states, full_w, preferred_element_type=F32).astype(BF16)  5.62 us
    reshape x1, local copies, waits for them, and re-layouts, shards(): keys = key_vectors.reshape(refl_rows, width)  2.54 us
  transfers between devices with their start and end apart: 1, of which 1 were waited for; matrix products, arithmetic and copies ran while one was open for 5% of the time, Pallas kernels for 43%

profile of v4, /device:TPU:0, one launch (start us, length us, event | category | flops | bytes accessed | tf_op | source)
XLA Modules:
  0.0 103.5 jit_solution(10315893567256901666)
XLA Ops:
  7.2 0.0 all-gather.2.cloned.1.call-start
  7.2 0.7 all-gather.2.cloned.1.call-update
  7.9 2.5 %reshape.22.k_ref = bf16[512,2048]{1,0:T(8,128)(2,1)S(1)} reshape(bf16[128,4,2048]{2,1,0:T(4,128)(2,1)} %param.6) | data formatting | bytes 4194304 | tf_op jit(solution)/shard_map/reshape | solution.py:203
  10.4 0.8 reshape.24
  11.2 0.1 fusion
  11.4 0.1 copy.14
  11.5 0.1 broadcast_in_dim.2
  11.5 0.1 copy.15
  11.6 0.9 copy.11
  12.6 0.1 copy.12
  12.7 0.0 copy-start
  12.7 1.0 copy-done
  13.7 0.0 copy-start.2
  13.7 0.0 copy-start.1
  13.7 35.7 %local.1 = (f32[16,128,128]{2,1,0:T(8,128)S(1)}, f32[16,1,128]{2,1,0:T(1,128)S(1)}, f32[16,4,128,128]{3,2,1,0:T(8,128)}, f32[16,4,128]{2,1,0:T(4,128)S(1)}) custom-call(bf16[512,2048]{1,0:T(8,128)(2,1)S(1)} %reshape.22.k_ref, f32[16,8,128]{2,1,0:T(8,128)S(1)} %pad_maximum_fusion.vec_ref, bf16[128,2048]{1,0:T(8,128)(2,1)S(1)} %copy-done), custom_call_target="tpu_custom_call" | custom-call | flops 12079595520 | bytes 10485760 | tf_op jit(solution)/shard_map/local/pallas_call | solution.py:224
  49.4 0.0 copy-done.2
  49.4 1.8 %chain.1 = f32[16,128]{1,0:T(8,128)S(1)} custom-call(f32[16,128,128]{2,1,0:T(8,128)S(1)} %get-tuple-element.8.map_ref, f32[16,1,128]{2,1,0:T(1,128)S(1)} %get-tuple-element.9.end_ref, f32[16,128]{1,0:T(8,128)S(1)} %bitcast.17), custom_call_target="tpu_custom_call" | custom-call | flops 60000000 | bytes 62914560 | tf_op jit(solution)/shard_map/chain/pallas_call | solution.py:242
  51.2 0.0 copy-done.1
  51.2 6.7 %states.1 = bf16[128,2048]{1,0:T(8,128)(2,1)} custom-call(bf16[512,2048]{1,0:T(8,128)(2,1)S(1)} %reshape.22.k_ref, f32[16,8,128]{2,1,0:T(8,128)S(1)} %pad_maximum_fusion.vec_ref, bf16[128,2048]{1,0:T(8,128)(2,1)S(1)} %copy-done.1, f32[16,4,128,128]{3,2,1,0:T(8,128)} %get-tuple-element.6.z_ref, f32[16,4,128]{2,1,0:T(4,128)S(1)} %get-tuple-element.7.z0_ref, ...), custom_call_target="tpu_custom_call" | custom-call | flops 1073741824 | bytes 10485760 | tf_op jit(solution)/shard_map/states/pallas_call | solution.py:260
  57.9 33.2 %all-gather.2.cloned.1.call-done = bf16[2048,2048]{1,0:T(8,128)(2,1)} async-done(((bf16[2048,128]{1,0:T(8,128)(2,1)}), bf16[2048,2048]{1,0:T(8,128)(2,1)}) %all-gather.2.cloned.1.call-update) | async-done | bytes 8388624 | tf_op jit(solution)/shard_map/all_gather | solution.py:216
  91.1 5.6 %convolution_convert_fusion = bf16[128,2048]{1,0:T(8,128)(2,1)} fusion(bf16[128,2048]{1,0:T(8,128)(2,1)} %states.1, bf16[2048,2048]{1,0:T(8,128)(2,1)} %all-gather.2.cloned.1.call-done), kind=kOutput, calls=%fused_computation | convolution fusion | flops 1074003968 | bytes 9437184 | tf_op jit(solution)/shard_map/dot_general | solution.py:279
  (2 shorter events, 0.0 us)
Async XLA Ops:
  7.2 83.9 %all-gather.2.cloned.1.call-start = ((), (), s32[]{:S(2)}) async-start(), calls=%async_computation | async-start | bytes 8912896 | tf_op jit(solution)/shard_map/all_gather | solution.py:216
  12.7 1.0 %copy-start = (bf16[128,2048]{1,0:T(8,128)(2,1)S(1)}, bf16[128,2048]{1,0:T(8,128)(2,1)}, u32[]{:S(2)}) copy-start(bf16[128,2048]{1,0:T(8,128)(2,1)} %v_ref.3) | copy-start | bytes 1572868
  13.7 35.7 %copy-start.2 = (f32[2048]{0:T(1024)S(1)}, f32[2048]{0:T(1024)}, u32[]{:S(2)}) copy-start(f32[2048]{0:T(1024)} %param.10) | copy-start | bytes 24580
  13.7 37.5 %copy-start.1 = (bf16[128,2048]{1,0:T(8,128)(2,1)S(1)}, bf16[128,2048]{1,0:T(8,128)(2,1)}, u32[]{:S(2)}) copy-start(bf16[128,2048]{1,0:T(8,128)(2,1)} %v_ref.3) | copy-start | bytes 1572868
Sparse Core Ops, SparseCore 0:
  10.2 80.8 all-gather.1

commit v5 on v4

--- a/solution.py
+++ b/solution.py
@@ -40,7 +40,7 @@
     return jnp.sum(jnp.where(eye, col, 0.0), axis=0, keepdims=True)
 
 
-def local_kernel(per, windows, k_ref, vec_ref, v_ref, map_ref, end_ref, z_ref, z0_ref):
+def local_kernel(per, windows, k_ref, vec_ref, v_ref, pack_ref, z_ref, z0_ref):
     i, j = iota((BS, BS), 0), iota((BS, BS), 1)
     eye = i == j
     eye_f = eye.astype(F32)
@@ -108,27 +108,36 @@
         for w in range(1, windows):
             end = jnp.sum(to_col(end, eye) * maps[b, w], axis=0, keepdims=True) + ends[b, w]
             total = dot3(split(total), split(maps[b, w]))
-        map_ref[b] = total
-        end_ref[b] = end
-
-
-def chain_kernel(axis, map_ref, end_ref, init_ref, out_ref, held, going, send_sem, recv_sem):
+        pack_ref[b, :BS, :] = total
+        pack_ref[b, BS:, :] = jnp.broadcast_to(end, (8, BS))
+
+
+def chain_kernel(axis, own_ref, sib_ref, init_ref, out_ref, held, going, pair, send_sem, recv_sem):
     blocks = init_ref.shape[0]
     count, me = lax.axis_size(axis), lax.axis_index(axis)
-    first, last = me == 0, me == count - 1
+    first, last = me < 2, me >= count - 2
+    odd = lax.rem(me, 2) == 1
     barrier = pltpu.get_barrier_semaphore()
 
     @pl.when(jnp.logical_not(first))
     def _():
         pl.semaphore_signal(
-            barrier, inc=1, device_id={axis: me - 1}, device_id_type=pl.DeviceIdType.MESH
+            barrier, inc=1, device_id={axis: me - 2}, device_id_type=pl.DeviceIdType.MESH
         )
 
     @pl.when(jnp.logical_not(last))
     def _():
         pl.semaphore_signal(
-            barrier, inc=1, device_id={axis: me + 1}, device_id_type=pl.DeviceIdType.MESH
-        )
+            barrier, inc=1, device_id={axis: me + 2}, device_id_type=pl.DeviceIdType.MESH
+        )
+
+    for b in range(blocks):
+        early = jnp.where(odd, sib_ref[b], own_ref[b])
+        late = jnp.where(odd, own_ref[b], sib_ref[b])
+        eye = iota((BS, BS), 0) == iota((BS, BS), 1)
+        pair[b, :BS, :] = dot3(split(early[:BS]), split(late[:BS]))
+        carried = jnp.sum(to_col(early[BS : BS + 1], eye) * late[:BS], axis=0, keepdims=True)
+        pair[b, BS:, :] = jnp.broadcast_to(carried + late[BS : BS + 1], (8, BS))
 
     pl.semaphore_wait(
         barrier, jnp.where(first, 0, 1).astype(jnp.int32) + jnp.where(last, 0, 1).astype(jnp.int32)
@@ -144,25 +153,35 @@
             device_id_type=pl.DeviceIdType.MESH,
         )
 
-    @pl.when(first)
-    def _():
-        out_ref[...] = init_ref[...]
-
-    @pl.when(jnp.logical_not(first))
-    def _():
-        copy(lax.rem(me + 1, count)).wait_recv()
-        out_ref[...] = held[...]
-
-    @pl.when(jnp.logical_not(last))
-    def _():
+    def push(source, target):
         columns = out_ref[...].T
         for b in range(blocks):
-            going[b : b + 1, :] = (
-                jnp.sum(columns[:, b : b + 1] * map_ref[b], axis=0, keepdims=True) + end_ref[b]
+            target[b : b + 1, :] = (
+                jnp.sum(columns[:, b : b + 1] * source[b, :BS, :], axis=0, keepdims=True)
+                + source[b, BS : BS + 1, :]
             )
-        sending = copy(me + 1)
-        sending.start()
-        sending.wait_send()
+
+    @pl.when(first)
+    def _():
+        out_ref[...] = init_ref[...]
+
+    @pl.when(jnp.logical_not(first))
+    def _():
+        copy(lax.rem(me + 2, count)).wait_recv()
+        out_ref[...] = held[...]
+
+    @pl.when(jnp.logical_not(last))
+    def _():
+        push(pair, going)
+        copy(me + 2).start()
+
+    @pl.when(odd)
+    def _():
+        push(sib_ref, out_ref)
+
+    @pl.when(jnp.logical_not(last))
+    def _():
+        copy(me + 2).wait_send()
 
 
 def states_kernel(per, windows, k_ref, vec_ref, v_ref, z_ref, z0_ref, x_ref, s_ref):
@@ -213,22 +232,25 @@
         ],
         axis=1,
     )
-    full_w = lax.all_gather(w_out, "tok", axis=1, tiled=True)
+    count = lax.axis_size("tok")
+    if count == 16:
+        order = [0, 1, 4, 5, 8, 9, 12, 13, 15, 14, 11, 10, 7, 6, 3, 2]
+    else:
+        order = list(range(0, count, 2)) + list(range(1, count, 2))[::-1]
+    full_w = lax.all_gather(w_out, "tok", axis=1, tiled=True, axis_index_groups=[order])
     vmem = 48 * 1024 * 1024
     key_spec = pl.BlockSpec((refl_rows, per * BS), lambda g: (0, g))
     vec_spec = pl.BlockSpec((per, 2 * windows, BS), lambda g: (g, 0, 0))
     row_spec = pl.BlockSpec((tok_rows, per * BS), lambda g: (0, g))
     z_spec = pl.BlockSpec((per, windows, BS, BS), lambda g: (g, 0, 0, 0))
     z0_spec = pl.BlockSpec((per, windows, BS), lambda g: (g, 0, 0))
-    vector_spec = pl.BlockSpec((per, 1, BS), lambda g: (g, 0, 0))
-    maps, ends, z, z0 = pl.pallas_call(
+    pack, z, z0 = pl.pallas_call(
         functools.partial(local_kernel, per, windows),
         grid=(blocks // per,),
         in_specs=[key_spec, vec_spec, row_spec],
-        out_specs=[pl.BlockSpec((per, BS, BS), lambda g: (g, 0, 0)), vector_spec, z_spec, z0_spec],
+        out_specs=[pl.BlockSpec((per, BS + 8, BS), lambda g: (g, 0, 0)), z_spec, z0_spec],
         out_shape=[
-            jax.ShapeDtypeStruct((blocks, BS, BS), F32),
-            jax.ShapeDtypeStruct((blocks, 1, BS), F32),
+            jax.ShapeDtypeStruct((blocks, BS + 8, BS), F32),
             jax.ShapeDtypeStruct((blocks, windows, BS, BS), F32),
             jax.ShapeDtypeStruct((blocks, windows, BS), F32),
         ],
@@ -239,6 +261,7 @@
         name="local",
     )(keys, vec, input_rows)
     whole = pl.BlockSpec(memory_space=pltpu.VMEM)
+    sibling = lax.ppermute(pack, "tok", [(at, at ^ 1) for at in range(count)])
     entry = pl.pallas_call(
         functools.partial(chain_kernel, "tok"),
         in_specs=[whole] * 3,
@@ -247,6 +270,7 @@
         scratch_shapes=[
             pltpu.VMEM((blocks, BS), F32),
             pltpu.VMEM((blocks, BS), F32),
+            pltpu.VMEM((blocks, BS + 8, BS), F32),
             pltpu.SemaphoreType.DMA,
             pltpu.SemaphoreType.DMA,
         ],
@@ -255,7 +279,7 @@
         ),
         cost_estimate=pl.CostEstimate(flops=60_000_000, bytes_accessed=60 << 20, transcendentals=0),
         name="chain",
-    )(maps, ends, init_state.reshape(blocks, BS))
+    )(pack, sibling, init_state.reshape(blocks, BS))
     more = 4
     states = pl.pallas_call(
         functools.partial(states_kernel, more, windows),
@@ -277,6 +301,14 @@
         name="states",
     )(keys, vec, input_rows, z, z0, entry.reshape(blocks, 1, BS))
     projected = jnp.dot(states, full_w, preferred_element_type=F32).astype(BF16)
+    wide = w_out.shape[1]
+    projected = jnp.concatenate(
+        [
+            projected[:, order.index(at) * wide : (order.index(at) + 1) * wide]
+            for at in range(count)
+        ],
+        axis=1,
+    )
     return (states, projected)
 
 

time: 104 us -> 92 us (0.88)
  the two profiles are of different devices: /device:TPU:0 before, /device:TPU:28 now
where the time goes in v5:
time: 92 us; the launch traced here: 91.7 us
  Pallas kernels  64.9 us (71%)
  between operations  14.2 us (15%)
  matrix products  4.97 us (5%)
  local copies, waits for them, and re-layouts  4.12 us (4%)
  waiting for transfers between devices  3.43 us (4%)
    pallas_call x1, Pallas kernels, shards(): pl.pallas_call(functools.partial(local_kernel, per, windows), grid=(block...  35.5 us
    pallas_call x1, Pallas kernels, shards(): pl.pallas_call(functools.partial(chain_kernel, 'tok'), in_specs=[whole] *...  22.7 us
    pallas_call x1, Pallas kernels, shards(): pl.pallas_call(functools.partial(states_kernel, more, windows), grid=(blo...  6.7 us
    dot_general x1, matrix products, shards(): projected = jnp.dot(states, full_w, preferred_element_type=F32).astype(BF16)  4.82 us
    ppermute x1, waiting for transfers between devices, shards(): sibling = lax.ppermute(pack, 'tok', [(at, at ^ 1) for at in range(count)])  2.75 us
    reshape x1, local copies, waits for them, and re-layouts, shards(): keys = key_vectors.reshape(refl_rows, width)  2.54 us
  transfers between devices with their start and end apart: 2, of which 1 were waited for; matrix products, arithmetic and copies ran while one was open for 4% of the time, Pallas kernels for 71%

profile of v5, /device:TPU:28, one launch (start us, length us, event | category | flops | bytes accessed | tf_op | source)
XLA Modules:
  0.0 91.7 jit_solution(17439094511188222459)
XLA Ops:
  7.2 0.0 copy-start.3
  7.2 0.0 copy-start.2
  7.2 0.0 copy-start
  7.2 0.0 all-gather.2.cloned.1.call-start
  7.2 0.7 all-gather.2.cloned.1.call-update
  7.9 2.5 %reshape.22.k_ref = bf16[512,2048]{1,0:T(8,128)(2,1)S(1)} reshape(bf16[128,4,2048]{2,1,0:T(4,128)(2,1)} %param.6) | data formatting | bytes 4194304 | tf_op jit(solution)/shard_map/reshape | solution.py:222
  10.5 0.0 copy-done.3
  10.5 0.1 reshape.24
  10.6 0.1 fusion
  10.7 0.1 copy.14
  10.8 0.1 broadcast_in_dim.2
  10.9 0.1 copy.15
  11.0 0.0 copy-done.2
  11.0 0.2 copy.11
  11.1 0.1 copy.12
  11.3 0.0 copy-start.1
  11.3 35.5 %local.1 = (f32[16,136,128]{2,1,0:T(8,128)S(1)}, f32[16,4,128,128]{3,2,1,0:T(8,128)}, f32[16,4,128]{2,1,0:T(4,128)S(1)}) custom-call(bf16[512,2048]{1,0:T(8,128)(2,1)S(1)} %reshape.22.k_ref, f32[16,8,128]{2,1,0:T(8,128)S(1)} %pad_maximum_fusion.vec_ref, bf16[128,2048]{1,0:T(8,128)(2,1)S(1)} %copy-done), custom_call_target="tpu_custom_call" | custom-call | flops 12079595520 | bytes 10485760 | tf_op jit(solution)/shard_map/local/pallas_call | solution.py:247
  46.8 0.0 collective-permute-start
  46.8 2.8 %collective-permute-done.sib_ref = f32[16,136,128]{2,1,0:T(8,128)S(1)} collective-permute-done((f32[16,136,128]{2,1,0:T(8,128)S(1)}, f32[16,136,128]{2,1,0:T(8,128)S(1)}, u32[]{:S(2)}, u32[]{:S(2)}) %collective-permute-start) | collective-permute-done | bytes 1114144 | tf_op jit(solution)/shard_map/ppermute | solution.py:264
  49.6 22.7 %chain.1 = f32[16,128]{1,0:T(8,128)S(1)} custom-call(f32[16,136,128]{2,1,0:T(8,128)S(1)} %get-tuple-element.7.own_ref, f32[16,136,128]{2,1,0:T(8,128)S(1)} %collective-permute-done.sib_ref, f32[16,128]{1,0:T(8,128)S(1)} %bitcast.17), custom_call_target="tpu_custom_call" | custom-call | flops 60000000 | bytes 62914560 | tf_op jit(solution)/shard_map/chain/pallas_call | solution.py:265
  72.3 6.7 %states.1 = bf16[128,2048]{1,0:T(8,128)(2,1)} custom-call(bf16[512,2048]{1,0:T(8,128)(2,1)S(1)} %reshape.22.k_ref, f32[16,8,128]{2,1,0:T(8,128)S(1)} %pad_maximum_fusion.vec_ref, bf16[128,2048]{1,0:T(8,128)(2,1)S(1)} %copy-done, f32[16,4,128,128]{3,2,1,0:T(8,128)} %get-tuple-element.5.z_ref, f32[16,4,128]{2,1,0:T(4,128)S(1)} %get-tuple-element.6.z0_ref, ...), custom_call_target="tpu_custom_call" | custom-call | flops 1073741824 | bytes 10485760 | tf_op jit(solution)/shard_map/states/pallas_call | solution.py:284
  79.0 4.8 %convolution_convert_fusion = bf16[128,2048]{1,0:T(8,128)(2,1)S(1)} fusion(bf16[128,2048]{1,0:T(8,128)(2,1)} %states.1, bf16[2048,2048]{1,0:T(8,128)(2,1)} %all-gather.2.cloned.1.call-done), kind=kOutput, calls=%fused_computation | convolution fusion | flops 1074003968 | bytes 9437184 | tf_op jit(solution)/shard_map/dot_general | solution.py:303
  84.1 0.0 copy-start.4
  84.1 0.8 copy-done.4
  (17 shorter events, 0.2 us)
Async XLA Ops:
  7.2 3.3 %copy-start.3 = (f32[128,16]{0,1:T(8,128)S(1)}, f32[128,16]{0,1:T(8,128)}, u32[]{:S(2)}) copy-start(f32[128,16]{0,1:T(8,128)} %param.8) | copy-start | bytes 24580
  7.2 3.8 %copy-start.2 = (f32[128,4,16]{0,2,1:T(8,128)S(1)}, f32[128,4,16]{0,2,1:T(8,128)}, u32[]{:S(2)}) copy-start(f32[128,4,16]{0,2,1:T(8,128)} %param.7) | copy-start | bytes 98308
  7.2 4.1 %copy-start = (bf16[128,2048]{1,0:T(8,128)(2,1)S(1)}, bf16[128,2048]{1,0:T(8,128)(2,1)}, u32[]{:S(2)}) copy-start(bf16[128,2048]{1,0:T(8,128)(2,1)} %v_ref.3) | copy-start | bytes 1572868
  7.2 71.8 %all-gather.2.cloned.1.call-start = ((), (), s32[]{:S(2)}) async-start(), calls=%async_computation | async-start | bytes 8912896 | tf_op jit(solution)/shard_map/all_gather | solution.py:240
  11.3 38.3 %copy-start.1 = (f32[2048]{0:T(1024)S(1)}, f32[2048]{0:T(1024)}, u32[]{:S(2)}) copy-start(f32[2048]{0:T(1024)} %param.10) | copy-start | bytes 24580
  46.8 2.8 %collective-permute-start = (f32[16,136,128]{2,1,0:T(8,128)S(1)}, f32[16,136,128]{2,1,0:T(8,128)S(1)}, u32[]{:S(2)}, u32[]{:S(2)}) collective-permute-start(f32[16,136,128]{2,1,0:T(8,128)S(1)} %get-tuple-element.7.own_ref), channel_id=1, source_target_pairs={{0,1},{1,0},{2,3},{3,2},{4,5},{5,4},{6,7},{7,6},{8,9},{9,8},{10,11... | collective-permute-start | bytes 3342344 | tf_op jit(solution)/shard_map/ppermute | solution.py:264
  84.1 0.8 copy-start.4
Sparse Core Ops, SparseCore 0:
  9.5 63.0 all-gather.1

commit v6 on v5

--- a/solution.py
+++ b/solution.py
@@ -218,7 +218,7 @@
     blocks = width // BS
     windows = tok_rows // WIN
     refl_rows = REFL * tok_rows
-    per = 2
+    per = 4
     keys = key_vectors.reshape(refl_rows, width)
     pos = jnp.arange(WIN)
     up_to = (pos[None, :] <= pos[:, None]).astype(F32)

time: 92 us -> 90 us (0.978); the launches traced: 91.7 us -> 88.8 us
  Pallas kernels: 64.9 us -> 62 us
    pallas_call x1, Pallas kernels: 35.5 us -> 32.5 us  [shards(): pl.pallas_call(functools.partial(local_kernel, per, windows), grid=(block...]
  transfers between devices with their start and end apart: 2 -> 2, of which waited for: 1 -> 1; matrix products, arithmetic and copies ran while one was open for 4% -> 4% of each run, Pallas kernels for 71% -> 70%
where the time goes in v6:
time: 90 us; the launch traced here: 88.8 us
  Pallas kernels  62 us (69%)
  between operations  14.2 us (16%)
  matrix products  4.97 us (6%)
  local copies, waits for them, and re-layouts  4.12 us (5%)
  waiting for transfers between devices  3.43 us (4%)
    pallas_call x1, Pallas kernels, shards(): pl.pallas_call(functools.partial(local_kernel, per, windows), grid=(block...  32.5 us
    pallas_call x1, Pallas kernels, shards(): pl.pallas_call(functools.partial(chain_kernel, 'tok'), in_specs=[whole] *...  22.8 us
    pallas_call x1, Pallas kernels, shards(): pl.pallas_call(functools.partial(states_kernel, more, windows), grid=(blo...  6.71 us
    dot_general x1, matrix products, shards(): projected = jnp.dot(states, full_w, preferred_element_type=F32).astype(BF16)  4.82 us
    ppermute x1, waiting for transfers between devices, shards(): sibling = lax.ppermute(pack, 'tok', [(at, at ^ 1) for at in range(count)])  2.75 us
    reshape x1, local copies, waits for them, and re-layouts, shards(): keys = key_vectors.reshape(refl_rows, width)  2.54 us
  transfers between devices with their start and end apart: 2, of which 1 were waited for; matrix products, arithmetic and copies ran while one was open for 4% of the time, Pallas kernels for 70%

profile of v6, /device:TPU:28, one launch (start us, length us, event | category | flops | bytes accessed | tf_op | source)
XLA Modules:
  0.0 88.8 jit_solution(6013609442078640381)
XLA Ops:
  7.2 0.0 copy-start.3
  7.2 0.0 copy-start.2
  7.2 0.0 copy-start
  7.2 0.0 all-gather.2.cloned.1.call-start
  7.2 0.7 all-gather.2.cloned.1.call-update
  7.9 2.5 %reshape.22.k_ref = bf16[512,2048]{1,0:T(8,128)(2,1)S(1)} reshape(bf16[128,4,2048]{2,1,0:T(4,128)(2,1)} %param.6) | data formatting | bytes 4194304 | tf_op jit(solution)/shard_map/reshape | solution.py:222
  10.5 0.0 copy-done.3
  10.5 0.1 reshape.24
  10.6 0.1 fusion
  10.7 0.1 copy.14
  10.8 0.1 broadcast_in_dim.2
  10.9 0.1 copy.15
  11.0 0.0 copy-done.2
  11.0 0.2 copy.11
  11.1 0.1 copy.12
  11.3 0.0 copy-start.1
  11.3 32.5 %local.1 = (f32[16,136,128]{2,1,0:T(8,128)S(1)}, f32[16,4,128,128]{3,2,1,0:T(8,128)}, f32[16,4,128]{2,1,0:T(4,128)S(1)}) custom-call(bf16[512,2048]{1,0:T(8,128)(2,1)S(1)} %reshape.22.k_ref, f32[16,8,128]{2,1,0:T(8,128)S(1)} %pad_maximum_fusion.vec_ref, bf16[128,2048]{1,0:T(8,128)(2,1)S(1)} %copy-done), custom_call_target="tpu_custom_call" | custom-call | flops 12079595520 | bytes 10485760 | tf_op jit(solution)/shard_map/local/pallas_call | solution.py:247
  43.8 0.0 collective-permute-start
  43.8 2.8 %collective-permute-done.sib_ref = f32[16,136,128]{2,1,0:T(8,128)S(1)} collective-permute-done((f32[16,136,128]{2,1,0:T(8,128)S(1)}, f32[16,136,128]{2,1,0:T(8,128)S(1)}, u32[]{:S(2)}, u32[]{:S(2)}) %collective-permute-start) | collective-permute-done | bytes 1114144 | tf_op jit(solution)/shard_map/ppermute | solution.py:264
  46.5 22.8 %chain.1 = f32[16,128]{1,0:T(8,128)S(1)} custom-call(f32[16,136,128]{2,1,0:T(8,128)S(1)} %get-tuple-element.7.own_ref, f32[16,136,128]{2,1,0:T(8,128)S(1)} %collective-permute-done.sib_ref, f32[16,128]{1,0:T(8,128)S(1)} %bitcast.17), custom_call_target="tpu_custom_call" | custom-call | flops 60000000 | bytes 62914560 | tf_op jit(solution)/shard_map/chain/pallas_call | solution.py:265
  69.3 6.7 %states.1 = bf16[128,2048]{1,0:T(8,128)(2,1)} custom-call(bf16[512,2048]{1,0:T(8,128)(2,1)S(1)} %reshape.22.k_ref, f32[16,8,128]{2,1,0:T(8,128)S(1)} %pad_maximum_fusion.vec_ref, bf16[128,2048]{1,0:T(8,128)(2,1)S(1)} %copy-done, f32[16,4,128,128]{3,2,1,0:T(8,128)} %get-tuple-element.5.z_ref, f32[16,4,128]{2,1,0:T(4,128)S(1)} %get-tuple-element.6.z0_ref, ...), custom_call_target="tpu_custom_call" | custom-call | flops 1073741824 | bytes 10485760 | tf_op jit(solution)/shard_map/states/pallas_call | solution.py:284
  76.0 4.8 %convolution_convert_fusion = bf16[128,2048]{1,0:T(8,128)(2,1)S(1)} fusion(bf16[128,2048]{1,0:T(8,128)(2,1)} %states.1, bf16[2048,2048]{1,0:T(8,128)(2,1)} %all-gather.2.cloned.1.call-done), kind=kOutput, calls=%fused_computation | convolution fusion | flops 1074003968 | bytes 9437184 | tf_op jit(solution)/shard_map/dot_general | solution.py:303
  81.1 0.0 copy-start.4
  81.2 0.8 copy-done.4
  (17 shorter events, 0.2 us)
Async XLA Ops:
  7.2 3.3 %copy-start.3 = (f32[128,16]{0,1:T(8,128)S(1)}, f32[128,16]{0,1:T(8,128)}, u32[]{:S(2)}) copy-start(f32[128,16]{0,1:T(8,128)} %param.8) | copy-start | bytes 24580
  7.2 3.8 %copy-start.2 = (f32[128,4,16]{0,2,1:T(8,128)S(1)}, f32[128,4,16]{0,2,1:T(8,128)}, u32[]{:S(2)}) copy-start(f32[128,4,16]{0,2,1:T(8,128)} %param.7) | copy-start | bytes 98308
  7.2 4.1 %copy-start = (bf16[128,2048]{1,0:T(8,128)(2,1)S(1)}, bf16[128,2048]{1,0:T(8,128)(2,1)}, u32[]{:S(2)}) copy-start(bf16[128,2048]{1,0:T(8,128)(2,1)} %v_ref.3) | copy-start | bytes 1572868
  7.2 68.8 %all-gather.2.cloned.1.call-start = ((), (), s32[]{:S(2)}) async-start(), calls=%async_computation | async-start | bytes 8912896 | tf_op jit(solution)/shard_map/all_gather | solution.py:240
  11.3 35.3 %copy-start.1 = (f32[2048]{0:T(1024)S(1)}, f32[2048]{0:T(1024)}, u32[]{:S(2)}) copy-start(f32[2048]{0:T(1024)} %param.10) | copy-start | bytes 24580
  43.8 2.8 %collective-permute-start = (f32[16,136,128]{2,1,0:T(8,128)S(1)}, f32[16,136,128]{2,1,0:T(8,128)S(1)}, u32[]{:S(2)}, u32[]{:S(2)}) collective-permute-start(f32[16,136,128]{2,1,0:T(8,128)S(1)} %get-tuple-element.7.own_ref), channel_id=1, source_target_pairs={{0,1},{1,0},{2,3},{3,2},{4,5},{5,4},{6,7},{7,6},{8,9},{9,8},{10,11... | collective-permute-start | bytes 3342344 | tf_op jit(solution)/shard_map/ppermute | solution.py:264
  81.1 0.8 copy-start.4
Sparse Core Ops, SparseCore 0:
  9.5 63.1 all-gather.1
